TPU v7x, 256 devices: a whole 4x4x8 slice. The times are simulated.
256 devices in a mesh: gx: 8 (over x, core), gy: 8 (over z), gz: 4 (over y).
Axes of the slice: x: 4, y: 4, z: 8, core: 2. Of those that a mesh axis runs over, the one named last changes fastest.
Arguments:
- vec_prev: float32 [2, 1024, 128, 512], P(None, 'gx', 'gy', 'gz'), may hold values from -4 to 4
- source: float32 [2, 1024, 128, 512], P(None, 'gx', 'gy', 'gz'), may hold values from -6 to 6
- mag_mat: int32 [1024, 128, 512], P('gx', 'gy', 'gz'), may hold values from 0 to 3
- send_idx: int32 [256, 64, 128], P(('gx', 'gy', 'gz')), may hold values from 0 to 262143
- send_count: int32 [256, 64], P(('gx', 'gy', 'gz')), may hold values from 1 to 128, as said below
- recv_cell: int32 [256, 64, 128], P(('gx', 'gy', 'gz')), may hold values from 0 to 131071
- temp: float32 [256, 128, 1024], P('gx', 'gy', 'gz'), may hold values from 0 to 2
- heat_mat: int32 [256, 128, 1024], P('gx', 'gy', 'gz'), may hold values from 0 to 3
Outputs:
- potential: float32 [2, 1024, 128, 512], P(None, 'gx', 'gy', 'gz')
- temp_out: float32 [256, 128, 1024], P('gx', 'gy', 'gz')
Inputs may be any that keep to these rules, and one draw needn't show every extreme that they name: `send_count`: in every draw one peer position receives 128 from every device.
All inputs are finite; a program needn't handle non-finite values.
Results may differ from a plain program's by a relative error of at most 0.00002.
Values sent between devices are 32-bit elements; how exact they have to be, the bound alone decides.
A program may use at most 128 MiB of HBM per device.

v0:
```python
import jax
import jax.numpy as jnp
from jax import lax
from jax.sharding import PartitionSpec as P

sigma_table = (0.0, 3.0, 1.5, 6.0)
conduct_table = (1.0, 0.15, 0.05, 0.9)
capacity_table = (7.0, 2.0, 1.0, 6.0)
upwind_rate = 0.3


def extended(block, sides, width):
    for axis, dim in sides:
        count = lax.axis_size(axis)
        forward = [(i, i + 1) for i in range(count - 1)]
        backward = [(target, source) for source, target in forward]
        low = lax.ppermute(
            lax.slice_in_dim(block, block.shape[dim] - width, None, axis=dim), axis, forward
        )
        high = lax.ppermute(lax.slice_in_dim(block, 0, width, axis=dim), axis, backward)
        block = jnp.concatenate([low, block, high], axis=dim)
    return block


def lookup(material, table):
    total = jnp.zeros(material.shape, jnp.float32)
    for number in range(4):
        total = total + jnp.where(material == number, jnp.float32(table[number]), jnp.float32(0.0))
    return total


def relax(padded, sigma, source):
    beside = padded[:, 2:, 1:-1, 1:-1] + padded[:, :-2, 1:-1, 1:-1]
    beside = beside + padded[:, 1:-1, 2:, 1:-1] + padded[:, 1:-1, :-2, 1:-1]
    beside = beside + padded[:, 1:-1, 1:-1, 2:] + padded[:, 1:-1, 1:-1, :-2]
    real_part = source[0] + beside[0]
    imag_part = source[1] + beside[1]
    denom = 36.0 + sigma * sigma
    return jnp.stack(
        [
            (6.0 * real_part + sigma * imag_part) / denom,
            (6.0 * imag_part - sigma * real_part) / denom,
        ]
    )


def heat_step(tpad, kpad, kcell, capacity, upwind, heat_src):
    center = tpad[1:-1, 1:-1, 1:-1]
    flux = jnp.zeros(center.shape, jnp.float32)
    shifts = [
        (slice(2, None), slice(1, -1), slice(1, -1)),
        (slice(None, -2), slice(1, -1), slice(1, -1)),
        (slice(1, -1), slice(2, None), slice(1, -1)),
        (slice(1, -1), slice(None, -2), slice(1, -1)),
        (slice(1, -1), slice(1, -1), slice(2, None)),
        (slice(1, -1), slice(1, -1), slice(None, -2)),
    ]
    for where_at in shifts:
        kside = kpad[where_at]
        face = 2.0 * kcell * kside / (kcell + kside)
        flux = flux + face * (tpad[where_at] - center)
    below = tpad[1:-1, 1:-1, :-2]
    return center + (flux + heat_src) / capacity + upwind * (below - center)


def split_index(flat_index, second, third):
    plane = second * third
    first_part = flat_index // plane
    rest = flat_index % plane
    return (first_part, rest // third, rest % third)


def shards(vec_prev, source, mag_mat, send_idx, send_count, recv_cell, temp, heat_mat):
    sigma = lookup(mag_mat, sigma_table)
    size_x, size_y, size_z = mag_mat.shape
    field = vec_prev
    for sweep in range(2):
        padded = extended(field, (("gx", 1), ("gy", 2), ("gz", 3)), 1)
        field = relax(padded, sigma, source)
    loss = 0.5 * sigma * (field[0] * field[0] + field[1] * field[1])
    slots = send_idx.shape[2]
    src_x, src_y, src_z = split_index(send_idx[0], size_y, size_z)
    values = loss[src_x, src_y, src_z]
    slot_mask = jnp.arange(slots, dtype=jnp.int32)[None, :] < send_count[0][:, None]
    values = jnp.where(slot_mask, values, jnp.float32(0.0))
    received = lax.all_to_all(values, ("gx", "gy"), split_axis=0, concat_axis=0, tiled=True)
    heat_x, heat_y, heat_z = temp.shape
    dst_x, dst_y, dst_z = split_index(recv_cell[0], heat_y, heat_z)
    heat_src = (
        jnp.zeros((heat_x, heat_y, heat_z), jnp.float32).at[dst_x, dst_y, dst_z].add(received)
    )
    kcell = lookup(heat_mat, conduct_table)
    capacity = lookup(heat_mat, capacity_table)
    upwind = jnp.where(heat_mat == 1, jnp.float32(upwind_rate), jnp.float32(0.0))
    kpad = extended(kcell, (("gx", 0), ("gy", 1), ("gz", 2)), 1)
    state = temp
    for step in range(3):
        tpad = extended(state, (("gx", 0), ("gy", 1), ("gz", 2)), 1)
        state = heat_step(tpad, kpad, kcell, capacity, upwind, heat_src)
    return (field, state)


def solution(mesh):
    placed = (
        P(None, "gx", "gy", "gz"),
        P(None, "gx", "gy", "gz"),
        P("gx", "gy", "gz"),
        P(("gx", "gy", "gz"), None, None),
        P(("gx", "gy", "gz"), None),
        P(("gx", "gy", "gz"), None, None),
        P("gx", "gy", "gz"),
        P("gx", "gy", "gz"),
    )
    return jax.shard_map(
        shards,
        mesh=mesh,
        in_specs=placed,
        out_specs=(P(None, "gx", "gy", "gz"), P("gx", "gy", "gz")),
        check_vma=False,
    )
```

profile of v0, /device:TPU:8, one launch (start us, length us, event | category | flops | bytes accessed | tf_op | source)
XLA Modules:
  0.0 394.1 jit_solution(12374015852031598354)
XLA Ops:
  4.6 2.2 select_add_fusion.2
  8.1 4.9 %collective-permute-start.14 = (f32[1,16,256]{2,1,0:T(8,128)S(1)}, f32[1,16,256]{2,1,0:T(8,128)S(1)}, u32[]{:S(2)}, u32[]{:S(2)}) collective-permute-start(f32[1,16,256]{2,1,0:T(8,128)S(1)} %get-tuple-element.44), channel_id=1, source_target_pairs={{0,32},{32,64},{64,96},{96,128},{128,160},{160,192},{192,224},{1,3... | collective-permute-start | bytes 49160 | tf_op jit(solution)/shard_map/ppermute | solution.py:17
  13.8 3.6 collective-permute-start.15
  24.8 4.6 %collective-permute-start.3 = (f32[2,130,1,128]{3,2,1,0:T(1,128)S(1)}, f32[2,130,1,128]{3,2,1,0:T(1,128)S(1)}, u32[]{:S(2)}, u32[]{:S(2)}) collective-permute-start(f32[2,130,1,128]{3,2,1,0:T(1,128)S(1)} %get-tuple-element.18), channel_id=1, source_target_pairs={{0,4},{4,8},{8,12},{12,16},{16,20},{20,24},{24,28},{1,5},{5,9},{9,... | collective-permute-start | bytes 399368 | tf_op jit(solution)/shard_map/ppermute | solution.py:17
  31.2 5.2 %collective-permute-start.18 = (f32[34,1,256]{2,1,0:T(1,128)S(1)}, f32[34,1,256]{2,1,0:T(1,128)}, u32[]{:S(2)}, u32[]{:S(2)}) collective-permute-start(f32[34,1,256]{2,1,0:T(1,128)S(1)} %get-tuple-element.36), channel_id=1, source_target_pairs={{0,4},{4,8},{8,12},{12,16},{16,20},{20,24},{24,28},{1,5},{5,9},{9,... | collective-permute-start | bytes 104456 | tf_op jit(solution)/shard_map/ppermute | solution.py:17
  38.5 5.2 %collective-permute-start.19 = (f32[34,1,256]{2,1,0:T(1,128)}, f32[34,1,256]{2,1,0:T(1,128)}, u32[]{:S(2)}, u32[]{:S(2)}) collective-permute-start(f32[34,1,256]{2,1,0:T(1,128)} %get-tuple-element.38), channel_id=1, source_target_pairs={{0,4},{4,8},{8,12},{12,16},{16,20},{20,24},{24,28},{1,5},{5,9},{9,... | collective-permute-start | bytes 104456 | tf_op jit(solution)/shard_map/ppermute | solution.py:17
  44.9 3.7 fusion.110
  48.6 4.7 %copy.10 = f32[2,130,18,1]{1,0,3,2:T(2,128)} copy(f32[2,130,18,1]{3,2,1,0:T(8,128)} %get-tuple-element.14) | data formatting | bytes 37440 | tf_op jit(solution)/shard_map/slice | solution.py:20
  53.3 2.4 collective-permute-start.4
  55.7 4.7 %copy.12 = f32[2,130,18,1]{1,0,3,2:T(2,128)} copy(f32[2,130,18,1]{3,2,1,0:T(8,128)} %get-tuple-element.15) | data formatting | bytes 37440 | tf_op jit(solution)/shard_map/slice | solution.py:18
  60.4 3.5 collective-permute-start.5
  64.8 4.3 %copy.11 = f32[2,130,18,1]{3,2,1,0:T(8,128)} copy(f32[2,130,18,1]{1,0,3,2:T(2,128)} %collective-permute-done.4) | data formatting | bytes 37440 | tf_op jit(solution)/shard_map/ppermute | solution.py:20
  69.1 4.4 %copy.13 = f32[2,130,18,1]{3,2,1,0:T(8,128)} copy(f32[2,130,18,1]{1,0,3,2:T(2,128)} %collective-permute-done.5) | data formatting | bytes 37440 | tf_op jit(solution)/shard_map/ppermute | solution.py:17
  73.5 5.8 %fusion.5 = f32[2,128,16,128]{3,2,1,0:T(8,128)S(1)} fusion(f32[2,130,18,1]{3,2,1,0:T(8,128)} %copy.13, f32[2,130,1,128]{3,2,1,0:T(1,128)} %copy-done.16, f32[2,130,16,128]{3,2,1,0:T(8,128)S(1)} %constant_dynamic-update-slice_fusion, f32[2,130,1,128]{3,2,1,0:T(1,128)} %copy-done.17, f32[2,130,18,1]{3,2,1,0:T(8,128)} %copy.11, f32[2,128,16,128]{3,2,1,0:T(8,128)} %param.8, ...), kind=kLoop, calls=%fused_computation.34 | loop fusion | flops 7864320 | bytes 6660672 | tf_op jit(solution)/shard_map/add | solution.py:35
  81.5 3.0 collective-permute-start.7
  85.6 2.9 collective-permute-start.20
  88.6 3.0 collective-permute-start.22
  93.2 4.7 %collective-permute-start.9 = (f32[2,130,1,128]{3,2,1,0:T(1,128)S(1)}, f32[2,130,1,128]{3,2,1,0:T(1,128)S(1)}, u32[]{:S(2)}, u32[]{:S(2)}) collective-permute-start(f32[2,130,1,128]{3,2,1,0:T(1,128)S(1)} %get-tuple-element.16), channel_id=1, source_target_pairs={{0,4},{4,8},{8,12},{12,16},{16,20},{20,24},{24,28},{1,5},{5,9},{9,... | collective-permute-start | bytes 399368 | tf_op jit(solution)/shard_map/ppermute | solution.py:17
  102.0 3.7 fusion.109
  105.6 4.7 %copy.14 = f32[2,130,18,1]{1,0,3,2:T(2,128)} copy(f32[2,130,18,1]{3,2,1,0:T(8,128)} %get-tuple-element.12) | data formatting | bytes 37440 | tf_op jit(solution)/shard_map/slice | solution.py:20
  110.4 3.1 collective-permute-start.10
  113.5 4.7 %copy.16 = f32[2,130,18,1]{1,0,3,2:T(2,128)} copy(f32[2,130,18,1]{3,2,1,0:T(8,128)} %get-tuple-element.13) | data formatting | bytes 37440 | tf_op jit(solution)/shard_map/slice | solution.py:18
  118.2 3.0 collective-permute-start.11
  121.3 2.2 fusion.116
  123.4 3.4 collective-permute-start.21
  126.9 2.4 collective-permute-start.23
  129.3 3.6 copy.15
  132.9 4.4 %copy.17 = f32[2,130,18,1]{3,2,1,0:T(8,128)} copy(f32[2,130,18,1]{1,0,3,2:T(2,128)} %collective-permute-done.11) | data formatting | bytes 37440 | tf_op jit(solution)/shard_map/ppermute | solution.py:17
  137.3 6.7 %fusion = f32[2,128,16,128]{3,2,1,0:T(8,128)S(1)} fusion(f32[2,130,18,1]{3,2,1,0:T(8,128)} %copy.17, f32[2,130,1,128]{3,2,1,0:T(1,128)} %copy-done.18, f32[2,130,1,128]{3,2,1,0:T(1,128)} %copy-done.19, f32[2,1,16,128]{3,2,1,0:T(8,128)S(1)} %copy-done.23, f32[2,1,16,128]{3,2,1,0:T(8,128)S(1)} %copy-done.25, f32[1,128,16,128]{3,2,1,0:T(8,128)S(1)} %get-tuple-element.11, ...), kind=kLoop, calls=%fused_computation.5 | loop fusion | flops 15204352 | bytes 4530752 | tf_op jit(solution)/shard_map/add | solution.py:35
  146.0 100.9 %gather_fusion = f32[8192]{0:T(1024)} fusion(f32[128,16,128]{2,1,0:T(8,128)S(1)} %get-tuple-element.7, s32[8192]{0:T(1024)S(1)} %fusion.92), kind=kCustom, calls=%fused_computation | custom fusion | bytes 163840 | tf_op jit(solution)/shard_map/gather | solution.py:83
  248.5 17.2 %all-to-all-start = ((f32[64,1,128]{2,1,0:T(1,128)}), f32[64,1,128]{2,1,0:T(1,128)S(1)}, u32[]{:S(2)}, u32[]{:S(2)}) async-start(f32[64,1,128]{2,1,0:T(1,128)} %compare_select_fusion), calls=%async_computation | async-start | bytes 65536 | tf_op jit(solution)/shard_map/all_to_all | solution.py:86
  266.4 8.7 %all-to-all-done = f32[64,1,128]{2,1,0:T(1,128)S(1)} async-done(((f32[64,1,128]{2,1,0:T(1,128)}), f32[64,1,128]{2,1,0:T(1,128)S(1)}, u32[]{:S(2)}, u32[]{:S(2)}) %all-to-all-start) | async-done | bytes 32800 | tf_op jit(solution)/shard_map/all_to_all | solution.py:86
  275.2 44.0 %scatter_custom_fusion = f32[131072]{0:T(1024)} fusion(s32[8192]{0:T(1024)S(1)} %select_bitcast_fusion, f32[8192]{0:T(1024)S(1)} %bitcast.90, f32[]{:T(128)} %constant.105.clone.1), kind=kCustom, calls=%fused_computation.211 | custom fusion | flops 8192 | bytes 524292
  320.4 5.4 %fusion.14 = f32[32,16,256]{2,1,0:T(8,128)S(1)} fusion(pred[32,16,256]{2,1,0:T(8,128)(4,1)} %get-tuple-element.6, f32[32,16,256]{2,1,0:T(8,128)} %param.14, f32[32,16,256]{2,1,0:T(8,128)S(1)} %reshape.464, f32[34,18,1]{2,1,0:T(8,128)} %collective-permute-done.21, f32[34,1,256]{2,1,0:T(1,128)} %collective-permute-done.17, f32[34,16,256]{2,1,0:T(8,128)S(1)} %copy-done.8, ...), kind=kLoop, calls=%fused_computation.71 | loop fusion | flops 10092544 | bytes 3393088 | tf_op jit(solution)/shard_map/add | solution.py:63
  327.3 3.0 collective-permute-start.25
  332.6 4.5 %collective-permute-start.27 = (f32[34,1,256]{2,1,0:T(1,128)S(1)}, f32[34,1,256]{2,1,0:T(1,128)S(1)}, u32[]{:S(2)}, u32[]{:S(2)}) collective-permute-start(f32[34,1,256]{2,1,0:T(1,128)S(1)} %get-tuple-element.34), channel_id=1, source_target_pairs={{0,4},{4,8},{8,12},{12,16},{16,20},{20,24},{24,28},{1,5},{5,9},{9,... | collective-permute-start | bytes 104456 | tf_op jit(solution)/shard_map/ppermute | solution.py:17
  339.0 3.8 collective-permute-start.28
  342.8 2.5 collective-permute-start.29
  345.4 7.7 %collective-permute-done.28 = f32[34,18,1]{2,1,0:T(8,128)S(1)} collective-permute-done((f32[34,18,1]{2,1,0:T(8,128)S(1)}, f32[34,18,1]{2,1,0:T(8,128)S(1)}, u32[]{:S(2)}, u32[]{:S(2)}) %collective-permute-start.28) | collective-permute-done | bytes 2480 | tf_op jit(solution)/shard_map/ppermute | solution.py:20
  353.0 2.8 collective-permute-done.29
  355.8 4.6 %fusion.15 = f32[32,16,256]{2,1,0:T(8,128)S(1)} fusion(pred[32,16,256]{2,1,0:T(8,128)(4,1)S(1)} %copy-done.13, f32[32,16,256]{2,1,0:T(8,128)S(1)} %fusion.14, f32[32,16,256]{2,1,0:T(8,128)S(1)} %reshape.464, f32[34,18,1]{2,1,0:T(8,128)S(1)} %collective-permute-done.28, f32[34,1,256]{2,1,0:T(1,128)S(1)} %collective-permute-done.26, ...), kind=kLoop, calls=%fused_computation.72 | loop fusion | flops 11141120 | bytes 2836032 | tf_op jit(solution)/shard_map/add | solution.py:63
  361.9 3.0 collective-permute-start.31
  367.1 4.9 %collective-permute-start.33 = (f32[34,1,256]{2,1,0:T(1,128)S(1)}, f32[34,1,256]{2,1,0:T(1,128)S(1)}, u32[]{:S(2)}, u32[]{:S(2)}) collective-permute-start(f32[34,1,256]{2,1,0:T(1,128)S(1)} %get-tuple-element.32), channel_id=1, source_target_pairs={{0,4},{4,8},{8,12},{12,16},{16,20},{20,24},{24,28},{1,5},{5,9},{9,... | collective-permute-start | bytes 104456 | tf_op jit(solution)/shard_map/ppermute | solution.py:17
  373.9 1.9 collective-permute-start.34
  375.9 3.9 collective-permute-start.35
  381.3 5.6 %collective-permute-done.34 = f32[34,18,1]{2,1,0:T(8,128)S(1)} collective-permute-done((f32[34,18,1]{2,1,0:T(8,128)S(1)}, f32[34,18,1]{2,1,0:T(8,128)S(1)}, u32[]{:S(2)}, u32[]{:S(2)}) %collective-permute-start.34) | collective-permute-done | bytes 2480 | tf_op jit(solution)/shard_map/ppermute | solution.py:20
  386.9 1.9 collective-permute-done.35
  388.8 5.3 %fusion.16 = f32[32,16,256]{2,1,0:T(8,128)} fusion(pred[32,16,256]{2,1,0:T(8,128)(4,1)S(1)} %copy-done.13, f32[32,16,256]{2,1,0:T(8,128)S(1)} %fusion.15, f32[32,16,256]{2,1,0:T(8,128)S(1)} %reshape.464, f32[34,18,1]{2,1,0:T(8,128)S(1)} %collective-permute-done.34, f32[34,1,256]{2,1,0:T(1,128)S(1)} %collective-permute-done.32, ...), kind=kLoop, calls=%fused_computation.73 | loop fusion | flops 11141120 | bytes 2836032 | tf_op jit(solution)/shard_map/add | solution.py:63
  (144 shorter events, 45.9 us)
Async XLA Ops:
  0.6 21.9 %copy-start = (f32[2,128,16,128]{3,2,1,0:T(8,128)S(1)}, f32[2,128,16,128]{3,2,1,0:T(8,128)}, u32[]{:S(2)}) copy-start(f32[2,128,16,128]{3,2,1,0:T(8,128)} %param.8) | copy-start | bytes 6291460
  1.5 19.6 %collective-permute-start.1 = (f32[2,1,16,128]{3,2,1,0:T(8,128)S(1)}, f32[2,1,16,128]{3,2,1,0:T(8,128)S(1)}, u32[]{:S(2)}, u32[]{:S(2)}) collective-permute-start(f32[2,1,16,128]{3,2,1,0:T(8,128)S(1)} %get-tuple-element.23), channel_id=1, source_target_pairs={{0,32},{32,64},{64,96},{96,128},{128,160},{160,192},{192,224},{1,3... | collective-permute-start | bytes 49160 | tf_op jit(solution)/shard_map/ppermute | solution.py:17
  3.3 19.4 %collective-permute-start = (f32[2,1,16,128]{3,2,1,0:T(8,128)S(1)}, f32[2,1,16,128]{3,2,1,0:T(8,128)S(1)}, u32[]{:S(2)}, u32[]{:S(2)}) collective-permute-start(f32[2,1,16,128]{3,2,1,0:T(8,128)S(1)} %get-tuple-element.22), channel_id=1, source_target_pairs={{32,0},{64,32},{96,64},{128,96},{160,128},{192,160},{224,192},{33,... | collective-permute-start | bytes 49160 | tf_op jit(solution)/shard_map/ppermute | solution.py:20
  6.8 18.0 %collective-permute-start.12 = (f32[1,16,256]{2,1,0:T(8,128)S(1)}, f32[1,16,256]{2,1,0:T(8,128)S(1)}, u32[]{:S(2)}, u32[]{:S(2)}) collective-permute-start(f32[1,16,256]{2,1,0:T(8,128)S(1)} %get-tuple-element.45), channel_id=1, source_target_pairs={{32,0},{64,32},{96,64},{128,96},{160,128},{192,160},{224,192},{33,... | collective-permute-start | bytes 49160 | tf_op jit(solution)/shard_map/ppermute | solution.py:20
  8.1 21.3 %collective-permute-start.14 = (f32[1,16,256]{2,1,0:T(8,128)S(1)}, f32[1,16,256]{2,1,0:T(8,128)S(1)}, u32[]{:S(2)}, u32[]{:S(2)}) collective-permute-start(f32[1,16,256]{2,1,0:T(8,128)S(1)} %get-tuple-element.44), channel_id=1, source_target_pairs={{0,32},{32,64},{64,96},{96,128},{128,160},{160,192},{192,224},{1,3... | collective-permute-start | bytes 49160 | tf_op jit(solution)/shard_map/ppermute | solution.py:17
  13.8 17.5 %collective-permute-start.15 = (f32[1,16,256]{2,1,0:T(8,128)S(1)}, f32[1,16,256]{2,1,0:T(8,128)S(1)}, u32[]{:S(2)}, u32[]{:S(2)}) collective-permute-start(f32[1,16,256]{2,1,0:T(8,128)S(1)} %get-tuple-element.47), channel_id=1, source_target_pairs={{0,32},{32,64},{64,96},{96,128},{128,160},{160,192},{192,224},{1,3... | collective-permute-start | bytes 49160 | tf_op jit(solution)/shard_map/ppermute | solution.py:17
  21.2 15.3 %collective-permute-start.13 = (f32[1,16,256]{2,1,0:T(8,128)S(1)}, f32[1,16,256]{2,1,0:T(8,128)S(1)}, u32[]{:S(2)}, u32[]{:S(2)}) collective-permute-start(f32[1,16,256]{2,1,0:T(8,128)S(1)} %get-tuple-element.46), channel_id=1, source_target_pairs={{32,0},{64,32},{96,64},{128,96},{160,128},{192,160},{224,192},{33,... | collective-permute-start | bytes 49160 | tf_op jit(solution)/shard_map/ppermute | solution.py:20
  23.5 15.1 %collective-permute-start.2 = (f32[2,130,1,128]{3,2,1,0:T(1,128)S(1)}, f32[2,130,1,128]{3,2,1,0:T(1,128)S(1)}, u32[]{:S(2)}, u32[]{:S(2)}) collective-permute-start(f32[2,130,1,128]{3,2,1,0:T(1,128)S(1)} %get-tuple-element.19), channel_id=1, source_target_pairs={{4,0},{8,4},{12,8},{16,12},{20,16},{24,20},{28,24},{5,1},{9,5},{13... | collective-permute-start | bytes 399368 | tf_op jit(solution)/shard_map/ppermute | solution.py:20
  24.8 19.0 %collective-permute-start.3 = (f32[2,130,1,128]{3,2,1,0:T(1,128)S(1)}, f32[2,130,1,128]{3,2,1,0:T(1,128)S(1)}, u32[]{:S(2)}, u32[]{:S(2)}) collective-permute-start(f32[2,130,1,128]{3,2,1,0:T(1,128)S(1)} %get-tuple-element.18), channel_id=1, source_target_pairs={{0,4},{4,8},{8,12},{12,16},{16,20},{20,24},{24,28},{1,5},{5,9},{9,... | collective-permute-start | bytes 399368 | tf_op jit(solution)/shard_map/ppermute | solution.py:17
  29.9 30.4 %collective-permute-start.16 = (f32[34,1,256]{2,1,0:T(1,128)S(1)}, f32[34,1,256]{2,1,0:T(1,128)S(1)}, u32[]{:S(2)}, u32[]{:S(2)}) collective-permute-start(f32[34,1,256]{2,1,0:T(1,128)S(1)} %get-tuple-element.37), channel_id=1, source_target_pairs={{4,0},{8,4},{12,8},{16,12},{20,16},{24,20},{28,24},{5,1},{9,5},{13... | collective-permute-start | bytes 104456 | tf_op jit(solution)/shard_map/ppermute | solution.py:20
  31.2 32.6 %collective-permute-start.18 = (f32[34,1,256]{2,1,0:T(1,128)S(1)}, f32[34,1,256]{2,1,0:T(1,128)}, u32[]{:S(2)}, u32[]{:S(2)}) collective-permute-start(f32[34,1,256]{2,1,0:T(1,128)S(1)} %get-tuple-element.36), channel_id=1, source_target_pairs={{0,4},{4,8},{8,12},{12,16},{16,20},{20,24},{24,28},{1,5},{5,9},{9,... | collective-permute-start | bytes 104456 | tf_op jit(solution)/shard_map/ppermute | solution.py:17
  37.2 55.9 %collective-permute-start.17 = (f32[34,1,256]{2,1,0:T(1,128)}, f32[34,1,256]{2,1,0:T(1,128)}, u32[]{:S(2)}, u32[]{:S(2)}) collective-permute-start(f32[34,1,256]{2,1,0:T(1,128)} %get-tuple-element.39), channel_id=1, source_target_pairs={{4,0},{8,4},{12,8},{16,12},{20,16},{24,20},{28,24},{5,1},{9,5},{13... | collective-permute-start | bytes 104456 | tf_op jit(solution)/shard_map/ppermute | solution.py:20
  38.5 59.4 %collective-permute-start.19 = (f32[34,1,256]{2,1,0:T(1,128)}, f32[34,1,256]{2,1,0:T(1,128)}, u32[]{:S(2)}, u32[]{:S(2)}) collective-permute-start(f32[34,1,256]{2,1,0:T(1,128)} %get-tuple-element.38), channel_id=1, source_target_pairs={{0,4},{4,8},{8,12},{12,16},{16,20},{20,24},{24,28},{1,5},{5,9},{9,... | collective-permute-start | bytes 104456 | tf_op jit(solution)/shard_map/ppermute | solution.py:17
  53.3 11.5 %collective-permute-start.4 = (f32[2,130,18,1]{1,0,3,2:T(2,128)}, f32[2,130,18,1]{1,0,3,2:T(2,128)}, u32[]{:S(2)}, u32[]{:S(2)}) collective-permute-start(f32[2,130,18,1]{1,0,3,2:T(2,128)} %copy.10), channel_id=1, source_target_pairs={{1,0},{2,1},{3,2},{5,4},{6,5},{7,6},{9,8},{10,9},{11,10},{13,12},{... | collective-permute-start | bytes 56168 | tf_op jit(solution)/shard_map/ppermute | solution.py:20
  60.4 8.7 %collective-permute-start.5 = (f32[2,130,18,1]{1,0,3,2:T(2,128)}, f32[2,130,18,1]{1,0,3,2:T(2,128)}, u32[]{:S(2)}, u32[]{:S(2)}) collective-permute-start(f32[2,130,18,1]{1,0,3,2:T(2,128)} %copy.12), channel_id=1, source_target_pairs={{0,1},{1,2},{2,3},{4,5},{5,6},{6,7},{8,9},{9,10},{10,11},{12,13},{... | collective-permute-start | bytes 56168 | tf_op jit(solution)/shard_map/ppermute | solution.py:17
  80.1 17.9 %copy-start.7 = (f32[34,16,256]{2,1,0:T(8,128)S(1)}, f32[34,16,256]{2,1,0:T(8,128)}, u32[]{:S(2)}) copy-start(f32[34,16,256]{2,1,0:T(8,128)} %copy-done.6) | copy-start | bytes 1671172
  80.1 8.5 %collective-permute-start.6 = (f32[2,1,16,128]{3,2,1,0:T(8,128)S(1)}, f32[2,1,16,128]{3,2,1,0:T(8,128)S(1)}, u32[]{:S(2)}, u32[]{:S(2)}) collective-permute-start(f32[2,1,16,128]{3,2,1,0:T(8,128)S(1)} %get-tuple-element.21), channel_id=1, source_target_pairs={{32,0},{64,32},{96,64},{128,96},{160,128},{192,160},{224,192},{33,... | collective-permute-start | bytes 49160 | tf_op jit(solution)/shard_map/ppermute | solution.py:20
  81.5 10.1 %collective-permute-start.7 = (f32[2,1,16,128]{3,2,1,0:T(8,128)S(1)}, f32[2,1,16,128]{3,2,1,0:T(8,128)S(1)}, u32[]{:S(2)}, u32[]{:S(2)}) collective-permute-start(f32[2,1,16,128]{3,2,1,0:T(8,128)S(1)} %get-tuple-element.20), channel_id=1, source_target_pairs={{0,32},{32,64},{64,96},{96,128},{128,160},{160,192},{192,224},{1,3... | collective-permute-start | bytes 49160 | tf_op jit(solution)/shard_map/ppermute | solution.py:17
  85.6 234.7 %collective-permute-start.20 = (f32[34,18,1]{2,1,0:T(8,128)}, f32[34,18,1]{2,1,0:T(8,128)S(1)}, u32[]{:S(2)}, u32[]{:S(2)}) collective-permute-start(f32[34,18,1]{2,1,0:T(8,128)} %get-tuple-element.29), channel_id=1, source_target_pairs={{1,0},{2,1},{3,2},{5,4},{6,5},{7,6},{9,8},{10,9},{11,10},{13,12},{... | collective-permute-start | bytes 7352 | tf_op jit(solution)/shard_map/ppermute | solution.py:20
  88.6 231.8 %collective-permute-start.22 = (f32[34,18,1]{2,1,0:T(8,128)}, f32[34,18,1]{2,1,0:T(8,128)S(1)}, u32[]{:S(2)}, u32[]{:S(2)}) collective-permute-start(f32[34,18,1]{2,1,0:T(8,128)} %get-tuple-element.28), channel_id=1, source_target_pairs={{0,1},{1,2},{2,3},{4,5},{5,6},{6,7},{8,9},{9,10},{10,11},{12,13},{... | collective-permute-start | bytes 7352 | tf_op jit(solution)/shard_map/ppermute | solution.py:17
  91.9 7.9 %collective-permute-start.8 = (f32[2,130,1,128]{3,2,1,0:T(1,128)S(1)}, f32[2,130,1,128]{3,2,1,0:T(1,128)S(1)}, u32[]{:S(2)}, u32[]{:S(2)}) collective-permute-start(f32[2,130,1,128]{3,2,1,0:T(1,128)S(1)} %get-tuple-element.17), channel_id=1, source_target_pairs={{4,0},{8,4},{12,8},{16,12},{20,16},{24,20},{28,24},{5,1},{9,5},{13... | collective-permute-start | bytes 399368 | tf_op jit(solution)/shard_map/ppermute | solution.py:20
  93.2 7.6 %collective-permute-start.9 = (f32[2,130,1,128]{3,2,1,0:T(1,128)S(1)}, f32[2,130,1,128]{3,2,1,0:T(1,128)S(1)}, u32[]{:S(2)}, u32[]{:S(2)}) collective-permute-start(f32[2,130,1,128]{3,2,1,0:T(1,128)S(1)} %get-tuple-element.16), channel_id=1, source_target_pairs={{0,4},{4,8},{8,12},{12,16},{16,20},{20,24},{24,28},{1,5},{5,9},{9,... | collective-permute-start | bytes 399368 | tf_op jit(solution)/shard_map/ppermute | solution.py:17
  110.4 16.5 %collective-permute-start.10 = (f32[2,130,18,1]{1,0,3,2:T(2,128)}, f32[2,130,18,1]{1,0,3,2:T(2,128)S(1)}, u32[]{:S(2)}, u32[]{:S(2)}) collective-permute-start(f32[2,130,18,1]{1,0,3,2:T(2,128)} %copy.14), channel_id=1, source_target_pairs={{1,0},{2,1},{3,2},{5,4},{6,5},{7,6},{9,8},{10,9},{11,10},{13,12},{... | collective-permute-start | bytes 56168 | tf_op jit(solution)/shard_map/ppermute | solution.py:20
  118.2 14.7 %collective-permute-start.11 = (f32[2,130,18,1]{1,0,3,2:T(2,128)}, f32[2,130,18,1]{1,0,3,2:T(2,128)}, u32[]{:S(2)}, u32[]{:S(2)}) collective-permute-start(f32[2,130,18,1]{1,0,3,2:T(2,128)} %copy.16), channel_id=1, source_target_pairs={{0,1},{1,2},{2,3},{4,5},{5,6},{6,7},{8,9},{9,10},{10,11},{12,13},{... | collective-permute-start | bytes 56168 | tf_op jit(solution)/shard_map/ppermute | solution.py:17
  123.4 197.0 %collective-permute-start.21 = (f32[34,18,1]{2,1,0:T(8,128)}, f32[34,18,1]{2,1,0:T(8,128)}, u32[]{:S(2)}, u32[]{:S(2)}) collective-permute-start(f32[34,18,1]{2,1,0:T(8,128)} %get-tuple-element.31), channel_id=1, source_target_pairs={{1,0},{2,1},{3,2},{5,4},{6,5},{7,6},{9,8},{10,9},{11,10},{13,12},{... | collective-permute-start | bytes 7352 | tf_op jit(solution)/shard_map/ppermute | solution.py:20
  126.9 193.5 %collective-permute-start.23 = (f32[34,18,1]{2,1,0:T(8,128)}, f32[34,18,1]{2,1,0:T(8,128)}, u32[]{:S(2)}, u32[]{:S(2)}) collective-permute-start(f32[34,18,1]{2,1,0:T(8,128)} %get-tuple-element.30), channel_id=1, source_target_pairs={{0,1},{1,2},{2,3},{4,5},{5,6},{6,7},{8,9},{9,10},{10,11},{12,13},{... | collective-permute-start | bytes 7352 | tf_op jit(solution)/shard_map/ppermute | solution.py:17
  146.0 100.9 %copy-start.30 = (s32[1,64]{1,0:T(1,128)S(1)}, s32[1,64]{1,0:T(1,128)}, u32[]{:S(2)}) copy-start(s32[1,64]{1,0:T(1,128)} %param.12) | copy-start | bytes 772
  146.0 174.4 %copy-start.15 = (f32[34,1,256]{2,1,0:T(1,128)S(1)}, f32[34,1,256]{2,1,0:T(1,128)}, u32[]{:S(2)}) copy-start(f32[34,1,256]{2,1,0:T(1,128)} %copy-done.14) | copy-start | bytes 104452
  246.9 73.5 %copy-start.8 = (f32[34,16,256]{2,1,0:T(8,128)S(1)}, f32[34,16,256]{2,1,0:T(8,128)}, u32[]{:S(2)}) copy-start(f32[34,16,256]{2,1,0:T(8,128)} %copy-done.6) | copy-start | bytes 1671172
  248.5 26.7 %all-to-all-start = ((f32[64,1,128]{2,1,0:T(1,128)}), f32[64,1,128]{2,1,0:T(1,128)S(1)}, u32[]{:S(2)}, u32[]{:S(2)}) async-start(f32[64,1,128]{2,1,0:T(1,128)} %compare_select_fusion), calls=%async_computation | async-start | bytes 65536 | tf_op jit(solution)/shard_map/all_to_all | solution.py:86
  325.8 30.0 %copy-start.10 = (pred[32,16,256]{2,1,0:T(8,128)(4,1)S(1)}, pred[32,16,256]{2,1,0:T(8,128)(4,1)}, u32[]{:S(2)}) copy-start(pred[32,16,256]{2,1,0:T(8,128)(4,1)} %get-tuple-element.3) | copy-start | bytes 393220
  325.9 30.0 %copy-start.11 = (pred[32,16,256]{2,1,0:T(8,128)(4,1)S(1)}, pred[32,16,256]{2,1,0:T(8,128)(4,1)}, u32[]{:S(2)}) copy-start(pred[32,16,256]{2,1,0:T(8,128)(4,1)} %get-tuple-element.4) | copy-start | bytes 393220
  325.9 29.9 %copy-start.12 = (pred[32,16,256]{2,1,0:T(8,128)(4,1)S(1)}, pred[32,16,256]{2,1,0:T(8,128)(4,1)}, u32[]{:S(2)}) copy-start(pred[32,16,256]{2,1,0:T(8,128)(4,1)} %get-tuple-element.5) | copy-start | bytes 393220
  325.9 29.9 %copy-start.13 = (pred[32,16,256]{2,1,0:T(8,128)(4,1)S(1)}, pred[32,16,256]{2,1,0:T(8,128)(4,1)}, u32[]{:S(2)}) copy-start(pred[32,16,256]{2,1,0:T(8,128)(4,1)} %get-tuple-element.6) | copy-start | bytes 393220
  325.9 29.9 %copy-start.21 = (f32[1,16,256]{2,1,0:T(8,128)S(1)}, f32[1,16,256]{2,1,0:T(8,128)}, u32[]{:S(2)}) copy-start(f32[1,16,256]{2,1,0:T(8,128)} %copy-done.20) | copy-start | bytes 49156
  325.9 4.5 %collective-permute-start.24 = (f32[1,16,256]{2,1,0:T(8,128)S(1)}, f32[1,16,256]{2,1,0:T(8,128)S(1)}, u32[]{:S(2)}, u32[]{:S(2)}) collective-permute-start(f32[1,16,256]{2,1,0:T(8,128)S(1)} %get-tuple-element.43), channel_id=1, source_target_pairs={{32,0},{64,32},{96,64},{128,96},{160,128},{192,160},{224,192},{33,... | collective-permute-start | bytes 49160 | tf_op jit(solution)/shard_map/ppermute | solution.py:20
  327.3 3.9 collective-permute-start.25
  331.3 6.2 %collective-permute-start.26 = (f32[34,1,256]{2,1,0:T(1,128)S(1)}, f32[34,1,256]{2,1,0:T(1,128)S(1)}, u32[]{:S(2)}, u32[]{:S(2)}) collective-permute-start(f32[34,1,256]{2,1,0:T(1,128)S(1)} %get-tuple-element.35), channel_id=1, source_target_pairs={{4,0},{8,4},{12,8},{16,12},{20,16},{24,20},{28,24},{5,1},{9,5},{13... | collective-permute-start | bytes 104456 | tf_op jit(solution)/shard_map/ppermute | solution.py:20
  332.6 6.2 %collective-permute-start.27 = (f32[34,1,256]{2,1,0:T(1,128)S(1)}, f32[34,1,256]{2,1,0:T(1,128)S(1)}, u32[]{:S(2)}, u32[]{:S(2)}) collective-permute-start(f32[34,1,256]{2,1,0:T(1,128)S(1)} %get-tuple-element.34), channel_id=1, source_target_pairs={{0,4},{4,8},{8,12},{12,16},{16,20},{20,24},{24,28},{1,5},{5,9},{9,... | collective-permute-start | bytes 104456 | tf_op jit(solution)/shard_map/ppermute | solution.py:17
  339.0 14.0 %collective-permute-start.28 = (f32[34,18,1]{2,1,0:T(8,128)S(1)}, f32[34,18,1]{2,1,0:T(8,128)S(1)}, u32[]{:S(2)}, u32[]{:S(2)}) collective-permute-start(f32[34,18,1]{2,1,0:T(8,128)S(1)} %get-tuple-element.27), channel_id=1, source_target_pairs={{1,0},{2,1},{3,2},{5,4},{6,5},{7,6},{9,8},{10,9},{11,10},{13,12},{... | collective-permute-start | bytes 7352 | tf_op jit(solution)/shard_map/ppermute | solution.py:20
  342.8 13.0 %collective-permute-start.29 = (f32[34,18,1]{2,1,0:T(8,128)S(1)}, f32[34,18,1]{2,1,0:T(8,128)S(1)}, u32[]{:S(2)}, u32[]{:S(2)}) collective-permute-start(f32[34,18,1]{2,1,0:T(8,128)S(1)} %get-tuple-element.26), channel_id=1, source_target_pairs={{0,1},{1,2},{2,3},{4,5},{5,6},{6,7},{8,9},{9,10},{10,11},{12,13},{... | collective-permute-start | bytes 7352 | tf_op jit(solution)/shard_map/ppermute | solution.py:17
  360.4 19.4 %copy-start.5 = (f32[128,16,128]{2,1,0:T(8,128)S(1)}, f32[128,16,128]{2,1,0:T(8,128)}, u32[]{:S(2)}) copy-start(f32[128,16,128]{2,1,0:T(8,128)} %get-tuple-element.9) | copy-start | bytes 3145732
  360.5 4.5 %collective-permute-start.30 = (f32[1,16,256]{2,1,0:T(8,128)S(1)}, f32[1,16,256]{2,1,0:T(8,128)S(1)}, u32[]{:S(2)}, u32[]{:S(2)}) collective-permute-start(f32[1,16,256]{2,1,0:T(8,128)S(1)} %get-tuple-element.41), channel_id=1, source_target_pairs={{32,0},{64,32},{96,64},{128,96},{160,128},{192,160},{224,192},{33,... | collective-permute-start | bytes 49160 | tf_op jit(solution)/shard_map/ppermute | solution.py:20
  361.9 3.9 collective-permute-start.31
  365.8 6.2 %collective-permute-start.32 = (f32[34,1,256]{2,1,0:T(1,128)S(1)}, f32[34,1,256]{2,1,0:T(1,128)S(1)}, u32[]{:S(2)}, u32[]{:S(2)}) collective-permute-start(f32[34,1,256]{2,1,0:T(1,128)S(1)} %get-tuple-element.33), channel_id=1, source_target_pairs={{4,0},{8,4},{12,8},{16,12},{20,16},{24,20},{28,24},{5,1},{9,5},{13... | collective-permute-start | bytes 104456 | tf_op jit(solution)/shard_map/ppermute | solution.py:20
  367.1 6.5 %collective-permute-start.33 = (f32[34,1,256]{2,1,0:T(1,128)S(1)}, f32[34,1,256]{2,1,0:T(1,128)S(1)}, u32[]{:S(2)}, u32[]{:S(2)}) collective-permute-start(f32[34,1,256]{2,1,0:T(1,128)S(1)} %get-tuple-element.32), channel_id=1, source_target_pairs={{0,4},{4,8},{8,12},{12,16},{16,20},{20,24},{24,28},{1,5},{5,9},{9,... | collective-permute-start | bytes 104456 | tf_op jit(solution)/shard_map/ppermute | solution.py:17
  373.9 12.9 %collective-permute-start.34 = (f32[34,18,1]{2,1,0:T(8,128)S(1)}, f32[34,18,1]{2,1,0:T(8,128)S(1)}, u32[]{:S(2)}, u32[]{:S(2)}) collective-permute-start(f32[34,18,1]{2,1,0:T(8,128)S(1)} %get-tuple-element.25), channel_id=1, source_target_pairs={{1,0},{2,1},{3,2},{5,4},{6,5},{7,6},{9,8},{10,9},{11,10},{13,12},{... | collective-permute-start | bytes 7352 | tf_op jit(solution)/shard_map/ppermute | solution.py:20
  375.9 12.9 %collective-permute-start.35 = (f32[34,18,1]{2,1,0:T(8,128)S(1)}, f32[34,18,1]{2,1,0:T(8,128)S(1)}, u32[]{:S(2)}, u32[]{:S(2)}) collective-permute-start(f32[34,18,1]{2,1,0:T(8,128)S(1)} %get-tuple-element.24), channel_id=1, source_target_pairs={{0,1},{1,2},{2,3},{4,5},{5,6},{6,7},{8,9},{9,10},{10,11},{12,13},{... | collective-permute-start | bytes 7352 | tf_op jit(solution)/shard_map/ppermute | solution.py:17
  (20 other events, 112.4 us)
where the time goes:
time: 396 us; the launch traced here: 394 us
  local copies, waits for them, and re-layouts  154 us (39%)
  starting transfers between devices  118 us (30%)
  other arithmetic  88.5 us (22%)
  waiting for transfers between devices  32.6 us (8%)
    gather x1, local copies, waits for them, and re-layouts, shards(): values = loss[src_x, src_y, src_z]  101 us
    ppermute x18, starting transfers between devices, extended(): lax.ppermute(lax.slice_in_dim(block, block.shape[dim] - width, None, axis...  66.9 us
    unnamed x4, other arithmetic  46.8 us
    ppermute x18, starting transfers between devices, extended(): lax.ppermute(lax.slice_in_dim(block, 0, width, axis=dim), axis, backward)  33.5 us
    slice x6, local copies, waits for them, and re-layouts, extended(): lax.slice_in_dim(block, 0, width, axis=dim)  18.4 us
    all_to_all x1, starting transfers between devices, shards(): lax.all_to_all(values, ('gx', 'gy'), split_axis=0, concat_axis=0, tiled=T...  17.2 us
    add x3, other arithmetic, heat_step(): return center + (flux + heat_src) / capacity + upwind * (below - center)  15.3 us
    slice x11, local copies, waits for them, and re-layouts, extended(): lax.slice_in_dim(block, block.shape[dim] - width, None, axis=dim)  14 us
  transfers between devices with their start and end apart: 37, of which 11 were waited for; matrix products, arithmetic and copies ran while one was open for 57% of the time, Pallas kernels for 0%

commit v1 on v0

v1 whole, which is shorter than its diff:
```python
import jax
import jax.numpy as jnp
from jax import lax
from jax.experimental import pallas as pl
from jax.experimental.pallas import tpu as pltpu
from jax.sharding import PartitionSpec as P

sigma_table = (0.0, 3.0, 1.5, 6.0)
conduct_table = (1.0, 0.15, 0.05, 0.9)
capacity_table = (7.0, 2.0, 1.0, 6.0)
upwind_rate = 0.3
real_table = tuple(6.0 / (36.0 + s * s) for s in sigma_table)
imag_table = tuple(s / (36.0 + s * s) for s in sigma_table)
inverse_capacity = tuple(1.0 / c for c in capacity_table)

MESH = pl.DeviceIdType.MESH
LANES = 128
AXES = ("gx", "gy", "gz")
f32 = jnp.float32
bf16 = jnp.bfloat16


def lookup(material, table):
    first = jnp.where(material == 0, f32(table[0]), f32(table[1]))
    second = jnp.where(material == 2, f32(table[2]), f32(table[3]))
    return jnp.where(material < 2, first, second)


def halves(value):
    high = value.astype(bf16)
    return high, (value - high.astype(f32)).astype(bf16)


class Exchange:
    def __init__(self, number, sends, receives, faces):
        self.number, self.sends, self.receives, self.faces = number, sends, receives, faces

    def each(self):
        for at, (axis, (low_face, high_face), (low_halo, high_halo)) in enumerate(self.faces):
            me, count = lax.axis_index(axis), lax.axis_size(axis)
            up = pltpu.make_async_remote_copy(
                src_ref=high_face, dst_ref=low_halo,
                send_sem=self.sends.at[self.number, 2 * at],
                recv_sem=self.receives.at[self.number, 2 * at],
                device_id={axis: lax.rem(me + 1, count)}, device_id_type=MESH,
            )
            down = pltpu.make_async_remote_copy(
                src_ref=low_face, dst_ref=high_halo,
                send_sem=self.sends.at[self.number, 2 * at + 1],
                recv_sem=self.receives.at[self.number, 2 * at + 1],
                device_id={axis: lax.rem(me + count - 1, count)}, device_id_type=MESH,
            )
            yield me > 0, me < count - 1, up, down, low_halo, high_halo

    def start(self, only=AXES):
        for (axis, _, _), (below, above, up, down, _, _) in zip(self.faces, self.each()):
            if axis in only:
                pl.when(above)(up.start)
                pl.when(below)(down.start)

    def wait(self):
        for below, above, up, down, low_halo, high_halo in self.each():
            pl.when(below)(up.wait_recv)
            pl.when(above)(down.wait_recv)

    def clear(self):
        for axis, _, (low_halo, high_halo) in self.faces:
            me, count = lax.axis_index(axis), lax.axis_size(axis)

            @pl.when(me == 0)
            def _():
                low_halo[...] = jnp.zeros(low_halo.shape, f32)

            @pl.when(me == count - 1)
            def _():
                high_halo[...] = jnp.zeros(high_halo.shape, f32)

    def drain(self):
        for below, above, up, down, _, _ in self.each():
            pl.when(above)(up.wait_send)
            pl.when(below)(down.wait_send)


def iota(shape, dim):
    return lax.broadcasted_iota(jnp.int32, shape, dim)


def to_column(face, x):
    low = pltpu.roll(face[:, :LANES], x, 1)
    high = pltpu.roll(face[:, face.shape[1] - LANES:], lax.rem(x + 1, LANES), 1)
    return low, high


def column_shifts(plane, low, high, x):
    rows, depth = plane.shape
    lane = iota((rows, depth), 1)
    before = pltpu.roll(low, lax.rem(LANES - x, LANES), 1)
    after = pltpu.roll(high, LANES - 1 - x, 1)
    if depth > LANES:
        before = jnp.concatenate([before] * (depth // LANES), axis=1)
        after = jnp.concatenate([after] * (depth // LANES), axis=1)
    return (
        jnp.where(lane == 0, before, pltpu.roll(plane, 1, 1)),
        jnp.where(lane == depth - 1, after, pltpu.roll(plane, depth - 1, 1)),
    )


def row_shifts(plane, low, high):
    rows, depth = plane.shape
    row = iota((rows, depth), 0)
    return (
        jnp.where(row == 0, low, pltpu.roll(plane, 1, 0)),
        jnp.where(row == rows - 1, high, pltpu.roll(plane, rows - 1, 0)),
    )


def kernel(
    vec_hbm, source_hbm, mag_hbm, idx_hbm, count_ref, cell_hbm, temp_hbm, heat_hbm,
    potential_hbm, out_hbm,
    field0, field1, source, mag, idx, cell, temp0, temp1, temp2, heat_mat, kcell, coef, rate,
    ys_m, yh_m, zs_m, zh_m, ys_t, yh_t, zs_t, zh_t,
    table, chosen, sent, landed, one_hot, v_high, v_low, heat,
    load_sems, halo_send, halo_recv, slot_send, slot_recv,
):
    _, size_x, size_y, size_z = source.shape
    heat_x, heat_y, heat_z = heat_mat.shape
    n_gx, n_gy = lax.axis_size("gx"), lax.axis_size("gy")
    ix, iy, iz, n_gz = lax.axis_index("gx"), lax.axis_index("gy"), lax.axis_index("gz"), lax.axis_size("gz")
    group, here = n_gx * n_gy, ix * n_gy + iy

    loads = [
        pltpu.make_async_copy(src, dst, load_sems.at[at])
        for at, (src, dst) in enumerate(
            [
                (vec_hbm, field0.at[:, pl.ds(1, size_x)]),
                (temp_hbm, temp0.at[pl.ds(1, heat_x)]),
                (heat_hbm, heat_mat),
                (mag_hbm, mag),
                (source_hbm, source),
                (idx_hbm.at[0], idx),
                (cell_hbm.at[0], cell),
            ]
        )
    ]
    for load in loads:
        load.start()

    barrier = pltpu.get_barrier_semaphore()

    @pl.loop(1, group)
    def _(step):
        peer = lax.rem(here + step, group)
        pl.semaphore_signal(
            barrier, inc=1, device_id={"gx": peer // n_gy, "gy": lax.rem(peer, n_gy)}, device_id_type=MESH
        )

    @pl.when(iz > 0)
    def _():
        pl.semaphore_signal(barrier, inc=1, device_id={"gz": lax.rem(iz + n_gz - 1, n_gz)}, device_id_type=MESH)

    @pl.when(iz < n_gz - 1)
    def _():
        pl.semaphore_signal(barrier, inc=1, device_id={"gz": lax.rem(iz + 1, n_gz)}, device_id_type=MESH)

    def faces(x_low, x_high, x_low_halo, x_high_halo, ys, yh, zs, zh, at):
        return [
            ("gx", (x_low, x_high), (x_low_halo, x_high_halo)),
            ("gy", (ys.at[at, 0], ys.at[at, 1]), (yh.at[at, 0], yh.at[at, 1])),
            ("gz", (zs.at[at, 0], zs.at[at, 1]), (zh.at[at, 0], zh.at[at, 1])),
        ]

    def mag_round(number, field, x_from):
        return Exchange(
            number, halo_send, halo_recv,
            faces(*x_from, field.at[:, 0], field.at[:, size_x + 1], ys_m, yh_m, zs_m, zh_m, number),
        )

    def heat_round(number, at, state):
        return Exchange(
            number, halo_send, halo_recv,
            faces(
                state.at[1], state.at[heat_x], state.at[0], state.at[heat_x + 1],
                ys_t, yh_t, zs_t, zh_t, at,
            ),
        )

    round0 = mag_round(0, field0, (vec_hbm.at[:, 0], vec_hbm.at[:, size_x - 1]))
    round1 = mag_round(1, field1, (field1.at[:, 1], field1.at[:, size_x]))
    round_t = heat_round(2, 0, temp0)
    round_k = heat_round(3, 1, kcell)
    round_1 = heat_round(4, 2, temp1)
    round_2 = heat_round(5, 3, temp2)
    rounds = (round0, round1, round_t, round_k, round_1, round_2)
    for each in rounds:
        each.clear()

    zero_m = jnp.zeros((size_y, LANES), f32)
    zero_t = jnp.zeros((heat_y, LANES), f32)
    lane_m = iota((size_y, LANES), 1)
    lane_t = iota((heat_y, LANES), 1)

    def pack_mag(at, x, planes, columns):
        result = []
        for part in range(2):
            ys_m[at, 0, part, x] = planes[part][0:1, :]
            ys_m[at, 1, part, x] = planes[part][size_y - 1:size_y, :]
            low, high = to_column(planes[part], x)
            result.append(jnp.where(lane_m == x, low, columns[2 * part]))
            result.append(jnp.where(lane_m == x, high, columns[2 * part + 1]))
        return tuple(result)

    def store_mag(at, columns):
        for part in range(2):
            zs_m[at, 0, part] = columns[2 * part]
            zs_m[at, 1, part] = columns[2 * part + 1]

    def pack_heat(at, x, plane, columns):
        ys_t[at, 0, x] = plane[0:1, :]
        ys_t[at, 1, x] = plane[heat_y - 1:heat_y, :]
        low, high = to_column(plane, x)
        return (
            jnp.where(lane_t == x, low, columns[0]),
            jnp.where(lane_t == x, high, columns[1]),
        )

    def store_heat(at, columns):
        zs_t[at, 0] = columns[0]
        zs_t[at, 1] = columns[1]

    loads[0].wait()
    columns = lax.fori_loop(
        0, size_x,
        lambda x, carry: pack_mag(0, x, (field0[0, x + 1], field0[1, x + 1]), carry),
        (zero_m,) * 4, unroll=4,
    )
    store_mag(0, columns)
    pl.semaphore_wait(barrier, group - 1 + (iz > 0).astype(jnp.int32) + (iz < n_gz - 1).astype(jnp.int32))
    round0.start()

    loads[1].wait()
    loads[2].wait()

    def pack_thermal(x, carry):
        conduct = lookup(heat_mat[x], conduct_table)
        kcell[x + 1] = conduct
        return pack_heat(0, x, temp0[x + 1], carry[:2]) + pack_heat(1, x, conduct, carry[2:])

    columns = lax.fori_loop(0, heat_x, pack_thermal, (zero_t,) * 4, unroll=4)
    store_heat(0, columns[:2])
    store_heat(1, columns[2:])
    round_t.start()
    round_k.start()
    for load in loads[3:]:
        load.wait()

    def relaxed(at, field, x, columns):
        total = []
        for part in range(2):
            plane = field[part, x + 1]
            low_y, high_y = row_shifts(plane, yh_m[at, 0, part, x], yh_m[at, 1, part, x])
            low_z, high_z = column_shifts(plane, columns[2 * part], columns[2 * part + 1], x)
            total.append(
                source[part, x] + ((field[part, x] + field[part, x + 2]) + (low_y + high_y) + (low_z + high_z))
            )
        material = mag[x]
        real, imag = lookup(material, real_table), lookup(material, imag_table)
        return real * total[0] + imag * total[1], real * total[1] - imag * total[0]

    def halo_columns(at):
        return (zh_m[at, 0, 0], zh_m[at, 1, 0], zh_m[at, 0, 1], zh_m[at, 1, 1])

    round0.wait()
    halo0 = halo_columns(0)

    def first_sweep(x, carry):
        planes = relaxed(0, field0, x, halo0)
        field1[0, x + 1] = planes[0]
        field1[1, x + 1] = planes[1]
        return pack_mag(1, x, planes, carry)

    store_mag(1, lax.fori_loop(0, size_x, first_sweep, (zero_m,) * 4, unroll=2))
    round1.start()

    round_t.wait()
    round_k.wait()

    def neighbours(at, state, x, columns):
        plane = state[x + 1]
        low_y, high_y = row_shifts(plane, yh_t[at, 0, x], yh_t[at, 1, x])
        low_z, high_z = column_shifts(plane, columns[0], columns[1], x)
        return plane, (state[x], state[x + 2], low_y, high_y, low_z, high_z)

    halo_k = (zh_t[1, 0], zh_t[1, 1])
    halo_t = (zh_t[0, 0], zh_t[0, 1])

    @pl.loop(0, heat_x)
    def _(x):
        material = heat_mat[x]
        conduct, beside = neighbours(1, kcell, x, halo_k)
        inverse = lookup(material, inverse_capacity)
        upwind = jnp.where(material == 1, f32(upwind_rate), f32(0.0))
        twice = (2.0 * inverse) * conduct
        centre = 1.0 - upwind
        weights = []
        for side, other in enumerate(beside):
            weight = twice * other / (conduct + other)
            centre = centre - weight
            if side == 4:
                weight = weight + upwind
            coef[side, x] = weight
            weights.append(weight)
        coef[6, x] = centre
        rate[x] = inverse
        plane, around = neighbours(0, temp0, x, halo_t)
        total = centre * plane
        for weight, other in zip(weights, around):
            total = total + weight * other
        temp1[x + 1] = total

    round1.wait()
    halo1 = halo_columns(1)
    block = LANES // size_y

    @pl.loop(0, size_x // block)
    def _(j):
        losses = []
        for i in range(block):
            x = j * block + i
            planes = relaxed(1, field1, x, halo1)
            field0[0, x + 1] = planes[0]
            field0[1, x + 1] = planes[1]
            losses.append(
                (0.5 * lookup(mag[x], sigma_table)) * (planes[0] * planes[0] + planes[1] * planes[1])
            )
        high, low = halves(jnp.transpose(jnp.concatenate(losses, axis=0)))
        at = pl.ds(pl.multiple_of(j * LANES, LANES), LANES)
        table[0:size_z, at] = high
        table[size_z:2 * size_z, at] = low

    store_potential = pltpu.make_async_copy(
        field0.at[:, pl.ds(1, size_x)], potential_hbm, load_sems.at[7]
    )
    store_potential.start()

    table_rows = size_x * size_y
    width = n_gy * LANES
    slot = iota((1, LANES), 1)
    row16 = lax.broadcasted_iota(jnp.int16, (table_rows, LANES), 0)
    sub_z = iota((size_z, LANES), 0)

    def slot_copy(peer, source_slot):
        return pltpu.make_async_remote_copy(
            src_ref=sent.at[peer], dst_ref=landed.at[source_slot],
            send_sem=slot_send.at[peer], recv_sem=slot_recv.at[source_slot],
            device_id={"gx": peer // n_gy, "gy": lax.rem(peer, n_gy)}, device_id_type=MESH,
        )

    @pl.loop(0, n_gx)
    def _(step):
        first = lax.rem(ix + step + 1, n_gx) * n_gy
        cells = []
        for p in range(n_gy):
            wanted = jnp.where(slot < count_ref[0, first + p], idx[pl.ds(first + p, 1), :], -1)
            cells.append(wanted)
            row = jnp.broadcast_to(lax.shift_right_arithmetic(wanted, 7).astype(jnp.int16), (table_rows, LANES))
            chosen[:, LANES * p:LANES * (p + 1)] = jnp.where(row16 == row, jnp.ones((), bf16), jnp.zeros((), bf16))
        found = jnp.dot(table[...], chosen[...], preferred_element_type=f32)
        found = found[:size_z] + found[size_z:]
        for p in range(n_gy):
            hit = sub_z == (cells[p] & (size_z - 1))
            sent[first + p] = jnp.sum(
                jnp.where(hit, found[:, LANES * p:LANES * (p + 1)], 0.0), axis=0, keepdims=True
            )
        for p in range(n_gy):
            @pl.when(first + p != here)
            def _():
                slot_copy(first + p, here).start()

    landed[here] = sent[here]

    row_h = lax.broadcasted_iota(jnp.int16, (heat_x * heat_y, LANES), 0)
    row_z = lax.broadcasted_iota(jnp.int16, (heat_z, LANES), 0)
    shift = heat_z.bit_length() - 1
    heat[...] = jnp.zeros(heat.shape, f32)
    per = one_hot.shape[1] // LANES
    zero16 = jnp.zeros((), bf16)
    transposed = (((1,), (1,)), ((), ()))

    @pl.loop(0, group // per)
    def _(step):
        for p in range(per):
            peer = step * per + p

            @pl.when(peer != here)
            def _():
                slot_copy(peer, peer).wait_recv()

        for p in range(per):
            peer = step * per + p
            target = cell[pl.ds(peer, 1), :]
            high, low = halves(landed[peer])
            at = slice(LANES * p, LANES * (p + 1))
            row = jnp.broadcast_to(lax.shift_right_logical(target, shift).astype(jnp.int16), row_h.shape)
            one_hot[:, at] = jnp.where(row_h == row, jnp.ones((), bf16), zero16)
            hit = row_z == jnp.broadcast_to((target & (heat_z - 1)).astype(jnp.int16), row_z.shape)
            v_high[:, at] = jnp.where(hit, jnp.broadcast_to(high, row_z.shape), zero16)
            v_low[:, at] = jnp.where(hit, jnp.broadcast_to(low, row_z.shape), zero16)
        heat[...] += lax.dot_general(
            one_hot[...], v_high[...], transposed, preferred_element_type=f32
        ) + lax.dot_general(one_hot[...], v_low[...], transposed, preferred_element_type=f32)

    def first_step(x, carry):
        gain = heat[pl.ds(pl.multiple_of(x * heat_y, heat_y), heat_y), :] * rate[x]
        rate[x] = gain
        plane = temp1[x + 1] + gain
        temp1[x + 1] = plane
        return pack_heat(2, x, plane, carry)

    store_heat(2, lax.fori_loop(0, heat_x, first_step, (zero_t,) * 2, unroll=2))
    round_1.start()
    round_t.drain()

    def stepped(at, state, x, columns):
        plane, around = neighbours(at, state, x, columns)
        total = coef[6, x] * plane + rate[x]
        for side, other in enumerate(around):
            total = total + coef[side, x] * other
        return total

    round_1.wait()
    halo_1 = (zh_t[2, 0], zh_t[2, 1])

    def second_step(x, carry):
        plane = stepped(2, temp1, x, halo_1)
        temp2[x + 1] = plane
        return pack_heat(3, x, plane, carry)

    store_heat(3, lax.fori_loop(0, heat_x, second_step, (zero_t,) * 2, unroll=2))
    round_2.start()
    round_2.wait()
    halo_2 = (zh_t[3, 0], zh_t[3, 1])

    @pl.loop(0, heat_x)
    def _(x):
        temp0[x + 1] = stepped(3, temp2, x, halo_2)

    store_temp = pltpu.make_async_copy(temp0.at[pl.ds(1, heat_x)], out_hbm, load_sems.at[8])
    store_temp.start()
    for each in (round0, round1, round_k, round_1, round_2):
        each.drain()

    @pl.loop(0, group)
    def _(peer):
        @pl.when(peer != here)
        def _():
            slot_copy(peer, here).wait_send()

    store_potential.wait()
    store_temp.wait()


def shards(vec_prev, source, mag_mat, send_idx, send_count, recv_cell, temp, heat_mat):
    _, size_x, size_y, size_z = vec_prev.shape
    heat_x, heat_y, heat_z = temp.shape
    n_gy = lax.axis_size("gy")
    group = lax.axis_size("gx") * n_gy
    per = min(16, group)
    vmem = pltpu.VMEM
    anywhere = pl.BlockSpec(memory_space=pl.ANY)
    return pl.pallas_call(
        kernel,
        out_shape=(
            jax.ShapeDtypeStruct(vec_prev.shape, f32),
            jax.ShapeDtypeStruct(temp.shape, f32),
        ),
        in_specs=[anywhere] * 4 + [pl.BlockSpec(memory_space=pltpu.SMEM)] + [anywhere] * 3,
        out_specs=(anywhere, anywhere),
        scratch_shapes=[
            vmem((2, size_x + 2, size_y, size_z), f32),
            vmem((2, size_x + 2, size_y, size_z), f32),
            vmem(source.shape, f32),
            vmem(mag_mat.shape, jnp.int32),
            vmem(send_idx.shape[1:], jnp.int32),
            vmem(recv_cell.shape[1:], jnp.int32),
            vmem((heat_x + 2, heat_y, heat_z), f32),
            vmem((heat_x + 2, heat_y, heat_z), f32),
            vmem((heat_x + 2, heat_y, heat_z), f32),
            vmem(heat_mat.shape, jnp.int32),
            vmem((heat_x + 2, heat_y, heat_z), f32),
            vmem((7, heat_x, heat_y, heat_z), f32),
            vmem((heat_x, heat_y, heat_z), f32),
            vmem((2, 2, 2, size_x, 1, size_z), f32),
            vmem((2, 2, 2, size_x, 1, size_z), f32),
            vmem((2, 2, 2, size_y, LANES), f32),
            vmem((2, 2, 2, size_y, LANES), f32),
            vmem((4, 2, heat_x, 1, heat_z), f32),
            vmem((4, 2, heat_x, 1, heat_z), f32),
            vmem((4, 2, heat_y, LANES), f32),
            vmem((4, 2, heat_y, LANES), f32),
            vmem((2 * size_z, size_x * size_y), bf16),
            vmem((size_x * size_y, n_gy * LANES), bf16),
            vmem((group, 1, LANES), f32),
            vmem((group, 1, LANES), f32),
            vmem((heat_x * heat_y, per * LANES), bf16),
            vmem((heat_z, per * LANES), bf16),
            vmem((heat_z, per * LANES), bf16),
            vmem((heat_x * heat_y, heat_z), f32),
            pltpu.SemaphoreType.DMA((9,)),
            pltpu.SemaphoreType.DMA((6, 6)),
            pltpu.SemaphoreType.DMA((6, 6)),
            pltpu.SemaphoreType.DMA((group,)),
            pltpu.SemaphoreType.DMA((group,)),
        ],
        compiler_params=pltpu.CompilerParams(
            collective_id=0, has_side_effects=True, vmem_limit_bytes=56 << 20
        ),
    )(vec_prev, source, mag_mat, send_idx, send_count, recv_cell, temp, heat_mat)


def solution(mesh):
    placed = (
        P(None, "gx", "gy", "gz"),
        P(None, "gx", "gy", "gz"),
        P("gx", "gy", "gz"),
        P(("gx", "gy", "gz"), None, None),
        P(("gx", "gy", "gz"), None),
        P(("gx", "gy", "gz"), None, None),
        P("gx", "gy", "gz"),
        P("gx", "gy", "gz"),
    )
    return jax.shard_map(
        shards,
        mesh=mesh,
        in_specs=placed,
        out_specs=(P(None, "gx", "gy", "gz"), P("gx", "gy", "gz")),
        check_vma=False,
    )
```

time: 396 us -> 79.2 us (0.20)
  local copies, waits for them, and re-layouts: 154 us -> 3.9 us
  starting transfers between devices: 118 us -> 0 us
  other arithmetic: 88.5 us -> 0 us
  Pallas kernels: 0 us -> 74.5 us
  waiting for transfers between devices: 32.6 us -> 0 us
    gather x1 -> x0, local copies, waits for them, and re-layouts: 101 us -> none  [shards(): values = loss[src_x, src_y, src_z]]
    ppermute x36 -> x0, starting transfers between devices: 100 us -> none  [the longest x18 66.9 us: extended(): lax.ppermute(lax.slice_in_dim(block, block.shape[dim] - width, None, axis...]
    pallas_call x0 -> x1, Pallas kernels: none -> 74.5 us  [shards(): pl.pallas_call(kernel, out_shape=(jax.ShapeDtypeStruct(vec_prev.shape, f3...]
    unnamed x4 -> x0, other arithmetic: 46.8 us -> none
    slice x17 -> x0, local copies, waits for them, and re-layouts: 32.4 us -> none  [the longest x6 18.4 us: extended(): lax.slice_in_dim(block, 0, width, axis=dim)]
    add x6 -> x0, other arithmetic: 30 us -> none  [the longest x3 15.3 us: heat_step(): return center + (flux + heat_src) / capacity + upwind * (below - center)]
    ppermute x36 -> x0, waiting for transfers between devices: 23.9 us -> none  [the longest x18 13.6 us: extended(): lax.ppermute(lax.slice_in_dim(block, 0, width, axis=dim), axis, backward)]
    all_to_all x1 -> x0, starting transfers between devices: 17.2 us -> none  [shards(): lax.all_to_all(values, ('gx', 'gy'), split_axis=0, concat_axis=0, tiled=T...]
  transfers between devices with their start and end apart: 37 -> 0, of which waited for: 11 -> 0; matrix products, arithmetic and copies ran while one was open for 57% -> 0% of each run, Pallas kernels for 0% -> 0%
where the time goes in v1:
time: 79.2 us; the launch traced here: 79.1 us
  Pallas kernels  74.5 us (94%)
  local copies, waits for them, and re-layouts  3.9 us (5%)
    pallas_call x1, Pallas kernels, shards(): pl.pallas_call(kernel, out_shape=(jax.ShapeDtypeStruct(vec_prev.shape, f3...  74.5 us
    unnamed x4, local copies, waits for them, and re-layouts  3.9 us

profile of v1, /device:TPU:8, one launch (start us, length us, event | category | flops | bytes accessed | tf_op | source)
XLA Modules:
  0.0 79.1 jit_solution(3556657088698751475)
XLA Ops:
  0.6 74.5 %shard_map.95 = (f32[2,128,16,128]{3,2,1,0:T(8,128)}, f32[32,16,256]{2,1,0:T(8,128)}) custom-call(f32[2,128,16,128]{3,2,1,0:T(8,128)} %vec_hbm.1, f32[2,128,16,128]{3,2,1,0:T(8,128)} %source_hbm.1, s32[128,16,128]{2,1,0:T(8,128)} %mag_hbm.1, s32[1,64,128]{2,1,0:T(8,128)} %idx_hbm.1, s32[1,64]{1,0:T(1,128)} %count_ref.1, s32[1,64,128]{2,1,0:T(8,128)} %cell_hbm.1, ...), custom_call_target="tpu_custom_call" | custom-call | tf_op jit(solution)/shard_map/pallas_call | solution.py:470
  75.2 0.0 copy-start
  75.2 3.1 %copy.12 = f32[2,128,16,128]{3,2,1,0:T(8,128)} copy(f32[2,128,16,128]{3,2,1,0:T(8,128)} %get-tuple-element.4) | data formatting | bytes 4194304
  78.3 0.0 copy-done
  78.3 0.8 %copy.13 = f32[32,16,256]{2,1,0:T(8,128)} copy(f32[32,16,256]{2,1,0:T(8,128)S(1)} %copy-done) | data formatting | bytes 1048576
Async XLA Ops:
  75.2 3.1 %copy-start = (f32[32,16,256]{2,1,0:T(8,128)S(1)}, f32[32,16,256]{2,1,0:T(8,128)}, u32[]{:S(2)}) copy-start(f32[32,16,256]{2,1,0:T(8,128)} %get-tuple-element.5) | copy-start | bytes 1572868

commit v2 on v1

v2 whole, which is shorter than its diff:
```python
import jax
import jax.numpy as jnp
from jax import lax
from jax.experimental import pallas as pl
from jax.experimental.pallas import tpu as pltpu
from jax.sharding import PartitionSpec as P

sigma_table = (0.0, 3.0, 1.5, 6.0)
conduct_table = (1.0, 0.15, 0.05, 0.9)
capacity_table = (7.0, 2.0, 1.0, 6.0)
upwind_rate = 0.3
real_table = tuple(6.0 / (36.0 + s * s) for s in sigma_table)
imag_table = tuple(s / (36.0 + s * s) for s in sigma_table)
inverse_capacity = tuple(1.0 / c for c in capacity_table)

MESH = pl.DeviceIdType.MESH
LANES = 128
AXES = ("gx", "gy", "gz")
f32 = jnp.float32
bf16 = jnp.bfloat16


def lookup(material, table):
    first = jnp.where(material == 0, f32(table[0]), f32(table[1]))
    second = jnp.where(material == 2, f32(table[2]), f32(table[3]))
    return jnp.where(material < 2, first, second)


def halves(value):
    high = value.astype(bf16)
    return high, (value - high.astype(f32)).astype(bf16)


class Exchange:
    def __init__(self, number, sends, receives, faces):
        self.number, self.sends, self.receives, self.faces = number, sends, receives, faces

    def each(self):
        for at, (axis, (low_face, high_face), (low_halo, high_halo)) in enumerate(self.faces):
            me, count = lax.axis_index(axis), lax.axis_size(axis)
            up = pltpu.make_async_remote_copy(
                src_ref=high_face, dst_ref=low_halo,
                send_sem=self.sends.at[self.number, 2 * at],
                recv_sem=self.receives.at[self.number, 2 * at],
                device_id={axis: wrap(me + 1, count)}, device_id_type=MESH,
            )
            down = pltpu.make_async_remote_copy(
                src_ref=low_face, dst_ref=high_halo,
                send_sem=self.sends.at[self.number, 2 * at + 1],
                recv_sem=self.receives.at[self.number, 2 * at + 1],
                device_id={axis: wrap(me + count - 1, count)}, device_id_type=MESH,
            )
            yield me > 0, me < count - 1, up, down, low_halo, high_halo

    def start(self, only=AXES):
        for (axis, _, _), (below, above, up, down, _, _) in zip(self.faces, self.each()):
            if axis in only:
                pl.when(above)(up.start)
                pl.when(below)(down.start)

    def wait(self):
        for below, above, up, down, low_halo, high_halo in self.each():
            pl.when(below)(up.wait_recv)
            pl.when(above)(down.wait_recv)

    def clear(self):
        for axis, _, (low_halo, high_halo) in self.faces:
            me, count = lax.axis_index(axis), lax.axis_size(axis)

            @pl.when(me == 0)
            def _():
                low_halo[...] = jnp.zeros(low_halo.shape, f32)

            @pl.when(me == count - 1)
            def _():
                high_halo[...] = jnp.zeros(high_halo.shape, f32)

    def drain(self):
        for below, above, up, down, _, _ in self.each():
            pl.when(above)(up.wait_send)
            pl.when(below)(down.wait_send)


def iota(shape, dim):
    return lax.broadcasted_iota(jnp.int32, shape, dim)


def wrap(value, count):
    return value & (count - 1) if count & (count - 1) == 0 else lax.rem(value, count)


def face_columns(planes):
    stacked = jnp.concatenate(planes, axis=0)
    depth = stacked.shape[1]
    low = jnp.transpose(stacked[:, :LANES])
    high = low if depth == LANES else jnp.transpose(stacked[:, depth - LANES:])
    return low[0:1, :], high[LANES - 1:LANES, :]


def halo_columns(low, high):
    sub = iota((LANES, LANES), 0)
    return jnp.transpose(jnp.where(sub == 0, low, jnp.where(sub == LANES - 1, high, f32(0.0))))


def column_shifts(plane, halo):
    rows, depth = plane.shape
    lane = iota((rows, depth), 1)
    if depth > LANES:
        halo = jnp.concatenate([halo] * (depth // LANES), axis=1)
    return (
        jnp.where(lane == 0, halo, pltpu.roll(plane, 1, 1)),
        jnp.where(lane == depth - 1, halo, pltpu.roll(plane, depth - 1, 1)),
    )


def row_shifts(plane, low, high):
    rows, depth = plane.shape
    row = iota((rows, depth), 0)
    return (
        jnp.where(row == 0, low, pltpu.roll(plane, 1, 0)),
        jnp.where(row == rows - 1, high, pltpu.roll(plane, rows - 1, 0)),
    )


def kernel(
    vec_hbm, source_hbm, mag_hbm, idx_hbm, count_hbm, cell_hbm, temp_hbm, heat_hbm,
    potential_hbm, out_hbm,
    field0, field1, source, mag, idx, count_ref, cell, temp0, temp1, temp2, heat_mat, kcell, coef, rate,
    ys_m, yh_m, zs_m, zh_m, ys_t, yh_t, zs_t, zh_t,
    table, chosen, sent, landed, one_hot, v_high, v_low, heat,
    load_sems, halo_send, halo_recv, slot_send, slot_recv,
):
    _, size_x, size_y, size_z = source.shape
    heat_x, heat_y, heat_z = heat_mat.shape
    n_gx, n_gy = lax.axis_size("gx"), lax.axis_size("gy")
    ix, iy, iz, n_gz = lax.axis_index("gx"), lax.axis_index("gy"), lax.axis_index("gz"), lax.axis_size("gz")
    group, here = n_gx * n_gy, ix * n_gy + iy

    loads = [
        pltpu.make_async_copy(src, dst, load_sems.at[at])
        for at, (src, dst) in enumerate(
            [
                (vec_hbm, field0.at[:, pl.ds(1, size_x)]),
                (temp_hbm, temp0.at[pl.ds(1, heat_x)]),
                (heat_hbm, heat_mat),
                (mag_hbm, mag),
                (source_hbm, source),
                (idx_hbm.at[0], idx),
                (cell_hbm.at[0], cell),
                (count_hbm, count_ref),
            ]
        )
    ]
    for load in loads:
        load.start()

    barrier = pltpu.get_barrier_semaphore()

    def greet(device):
        pl.semaphore_signal(barrier, inc=1, device_id=device, device_id_type=MESH)

    for step in range(1, n_gy):
        greet({"gy": wrap(iy + step, n_gy)})

    @pl.loop(1, n_gx)
    def _(step):
        for other in range(n_gy):
            greet({"gx": wrap(ix + step, n_gx), "gy": other})

    @pl.when(iz > 0)
    def _():
        greet({"gz": wrap(iz + n_gz - 1, n_gz)})

    @pl.when(iz < n_gz - 1)
    def _():
        greet({"gz": wrap(iz + 1, n_gz)})

    def faces(x_low, x_high, x_low_halo, x_high_halo, ys, yh, zs, zh, at):
        return [
            ("gx", (x_low, x_high), (x_low_halo, x_high_halo)),
            ("gy", (ys.at[at, 0], ys.at[at, 1]), (yh.at[at, 0], yh.at[at, 1])),
            ("gz", (zs.at[at, 0], zs.at[at, 1]), (zh.at[at, 0], zh.at[at, 1])),
        ]

    def mag_round(number, field, x_from):
        return Exchange(
            number, halo_send, halo_recv,
            faces(*x_from, field.at[:, 0], field.at[:, size_x + 1], ys_m, yh_m, zs_m, zh_m, number),
        )

    def heat_round(number, at, state):
        return Exchange(
            number, halo_send, halo_recv,
            faces(
                state.at[1], state.at[heat_x], state.at[0], state.at[heat_x + 1],
                ys_t, yh_t, zs_t, zh_t, at,
            ),
        )

    round0 = mag_round(0, field0, (vec_hbm.at[:, 0], vec_hbm.at[:, size_x - 1]))
    round1 = mag_round(1, field1, (field1.at[:, 1], field1.at[:, size_x]))
    round_t = heat_round(2, 0, temp0)
    round_k = heat_round(3, 1, kcell)
    round_1 = heat_round(4, 2, temp1)
    round_2 = heat_round(5, 3, temp2)
    rounds = (round0, round1, round_t, round_k, round_1, round_2)
    for each in rounds:
        each.clear()

    block = LANES // size_y
    block_t = LANES // heat_y

    def pack_mag(at, j, part, planes):
        for i, plane in enumerate(planes):
            ys_m[at, 0, part, j * block + i] = plane[0:1, :]
            ys_m[at, 1, part, j * block + i] = plane[size_y - 1:size_y, :]
        zs_m[at, 0, part, j], zs_m[at, 1, part, j] = face_columns(planes)

    def pack_heat(at, j, planes):
        for i, plane in enumerate(planes):
            ys_t[at, 0, j * block_t + i] = plane[0:1, :]
            ys_t[at, 1, j * block_t + i] = plane[heat_y - 1:heat_y, :]
        zs_t[at, 0, j], zs_t[at, 1, j] = face_columns(planes)

    loads[0].wait()

    @pl.loop(0, size_x // block)
    def _(j):
        for part in range(2):
            pack_mag(0, j, part, [field0[part, j * block + i + 1] for i in range(block)])

    pl.semaphore_wait(barrier, group - 1 + (iz > 0).astype(jnp.int32) + (iz < n_gz - 1).astype(jnp.int32))
    round0.start()

    loads[1].wait()
    loads[2].wait()

    @pl.loop(0, heat_x // block_t)
    def _(j):
        planes = []
        for i in range(block_t):
            x = j * block_t + i
            planes.append(lookup(heat_mat[x], conduct_table))
            kcell[x + 1] = planes[-1]
        pack_heat(1, j, planes)
        pack_heat(0, j, [temp0[j * block_t + i + 1] for i in range(block_t)])

    round_t.start()
    round_k.start()
    for load in loads[3:]:
        load.wait()

    def relaxed(at, field, j):
        columns = [halo_columns(zh_m[at, 0, part, j], zh_m[at, 1, part, j]) for part in range(2)]
        result = ([], [])
        for i in range(block):
            x = j * block + i
            total = []
            for part in range(2):
                plane = field[part, x + 1]
                low_y, high_y = row_shifts(plane, yh_m[at, 0, part, x], yh_m[at, 1, part, x])
                low_z, high_z = column_shifts(plane, columns[part][i * size_y:(i + 1) * size_y, :])
                total.append(
                    source[part, x] + ((field[part, x] + field[part, x + 2]) + (low_y + high_y) + (low_z + high_z))
                )
            material = mag[x]
            real, imag = lookup(material, real_table), lookup(material, imag_table)
            result[0].append(real * total[0] + imag * total[1])
            result[1].append(real * total[1] - imag * total[0])
        return result

    round0.wait()

    @pl.loop(0, size_x // block)
    def _(j):
        for part, planes in enumerate(relaxed(0, field0, j)):
            for i, plane in enumerate(planes):
                field1[part, j * block + i + 1] = plane
            pack_mag(1, j, part, planes)

    round1.start()

    round_t.wait()
    round_k.wait()

    def neighbours(at, state, j):
        columns = halo_columns(zh_t[at, 0, j], zh_t[at, 1, j])
        for i in range(block_t):
            x = j * block_t + i
            plane = state[x + 1]
            low_y, high_y = row_shifts(plane, yh_t[at, 0, x], yh_t[at, 1, x])
            low_z, high_z = column_shifts(plane, columns[i * heat_y:(i + 1) * heat_y, :])
            yield x, plane, (state[x], state[x + 2], low_y, high_y, low_z, high_z)

    @pl.loop(0, heat_x // block_t)
    def _(j):
        for (x, conduct, beside), (_, plane, around) in zip(neighbours(1, kcell, j), neighbours(0, temp0, j)):
            material = heat_mat[x]
            inverse = lookup(material, inverse_capacity)
            upwind = jnp.where(material == 1, f32(upwind_rate), f32(0.0))
            twice = (2.0 * inverse) * conduct
            centre = 1.0 - upwind
            total = jnp.zeros(plane.shape, f32)
            for side in range(6):
                weight = twice * beside[side] / (conduct + beside[side])
                centre = centre - weight
                if side == 4:
                    weight = weight + upwind
                coef[side, x] = weight
                total = total + weight * around[side]
            coef[6, x] = centre
            rate[x] = inverse
            temp1[x + 1] = total + centre * plane

    round1.wait()

    @pl.loop(0, size_x // block)
    def _(j):
        losses = []
        for i, planes in enumerate(zip(*relaxed(1, field1, j))):
            x = j * block + i
            field0[0, x + 1] = planes[0]
            field0[1, x + 1] = planes[1]
            losses.append(
                (0.5 * lookup(mag[x], sigma_table)) * (planes[0] * planes[0] + planes[1] * planes[1])
            )
        high, low = halves(jnp.transpose(jnp.concatenate(losses, axis=0)))
        at = pl.ds(pl.multiple_of(j * LANES, LANES), LANES)
        table[0:size_z, at] = high
        table[size_z:2 * size_z, at] = low

    store_potential = pltpu.make_async_copy(
        field0.at[:, pl.ds(1, size_x)], potential_hbm, load_sems.at[8]
    )
    store_potential.start()

    table_rows = size_x * size_y
    width = n_gy * LANES
    slot = iota((1, LANES), 1)
    row16 = lax.broadcasted_iota(jnp.int16, (table_rows, LANES), 0)
    sub_z = iota((size_z, LANES), 0)

    def slot_copy(gx, gy):
        return pltpu.make_async_remote_copy(
            src_ref=sent.at[gx * n_gy + gy], dst_ref=landed.at[here],
            send_sem=slot_send, recv_sem=slot_recv.at[ix],
            device_id={"gx": gx, "gy": gy}, device_id_type=MESH,
        )

    def slots_from(gx, count):
        rows = landed.at[pl.ds(gx * n_gy, count)]
        return pltpu.make_async_remote_copy(
            src_ref=rows, dst_ref=rows, send_sem=slot_send, recv_sem=slot_recv.at[gx],
            device_id={"gx": wrap(ix + 1, n_gx)}, device_id_type=MESH,
        )

    @pl.loop(0, n_gx)
    def _(step):
        target = wrap(ix + step + 1, n_gx)
        first = target * n_gy
        cells = []
        for p in range(n_gy):
            wanted = jnp.where(slot < count_ref[0, first + p], idx[pl.ds(first + p, 1), :], -1)
            cells.append(wanted)
            row = jnp.broadcast_to(lax.shift_right_arithmetic(wanted, 7).astype(jnp.int16), (table_rows, LANES))
            chosen[:, LANES * p:LANES * (p + 1)] = jnp.where(row16 == row, jnp.ones((), bf16), jnp.zeros((), bf16))
        found = jnp.dot(table[...], chosen[...], preferred_element_type=f32)
        found = found[:size_z] + found[size_z:]
        for p in range(n_gy):
            hit = sub_z == (cells[p] & (size_z - 1))
            sent[first + p] = jnp.sum(
                jnp.where(hit, found[:, LANES * p:LANES * (p + 1)], 0.0), axis=0, keepdims=True
            )
        for p in range(n_gy):
            @pl.when(first + p != here)
            def _():
                slot_copy(target, p).start()

    landed[here] = sent[here]

    row_h = lax.broadcasted_iota(jnp.int16, (heat_x * heat_y, LANES), 0)
    row_z = lax.broadcasted_iota(jnp.int16, (heat_z, LANES), 0)
    shift = heat_z.bit_length() - 1
    heat[...] = jnp.zeros(heat.shape, f32)
    per = one_hot.shape[1] // LANES // n_gy
    zero16 = jnp.zeros((), bf16)
    transposed = (((1,), (1,)), ((), ()))

    @pl.loop(0, n_gx // per)
    def _(step):
        peers = []
        for k in range(per):
            gx = wrap(ix + 2 * n_gx - 1 - (step * per + k), n_gx)

            @pl.when(gx != ix)
            def _():
                slots_from(gx, n_gy).wait_recv()

            @pl.when(gx == ix)
            def _():
                slots_from(gx, n_gy - 1).wait_recv()

            peers += [gx * n_gy + gy for gy in range(n_gy)]

        for p, peer in enumerate(peers):
            target = cell[pl.ds(peer, 1), :]
            high, low = halves(landed[peer])
            at = slice(LANES * p, LANES * (p + 1))
            row = jnp.broadcast_to(lax.shift_right_logical(target, shift).astype(jnp.int16), row_h.shape)
            one_hot[:, at] = jnp.where(row_h == row, jnp.ones((), bf16), zero16)
            hit = row_z == jnp.broadcast_to((target & (heat_z - 1)).astype(jnp.int16), row_z.shape)
            v_high[:, at] = jnp.where(hit, jnp.broadcast_to(high, row_z.shape), zero16)
            v_low[:, at] = jnp.where(hit, jnp.broadcast_to(low, row_z.shape), zero16)
        heat[...] += lax.dot_general(
            one_hot[...], v_high[...], transposed, preferred_element_type=f32
        ) + lax.dot_general(one_hot[...], v_low[...], transposed, preferred_element_type=f32)

    @pl.loop(0, heat_x // block_t)
    def _(j):
        planes = []
        for i in range(block_t):
            x = j * block_t + i
            gain = heat[pl.ds(pl.multiple_of(x * heat_y, heat_y), heat_y), :] * rate[x]
            rate[x] = gain
            planes.append(temp1[x + 1] + gain)
            temp1[x + 1] = planes[-1]
        pack_heat(2, j, planes)

    round_1.start()
    round_t.drain()

    def stepped(at, state, j):
        for x, plane, around in neighbours(at, state, j):
            total = coef[6, x] * plane + rate[x]
            for side, other in enumerate(around):
                total = total + coef[side, x] * other
            yield x, total

    round_1.wait()

    @pl.loop(0, heat_x // block_t)
    def _(j):
        planes = []
        for x, plane in stepped(2, temp1, j):
            temp2[x + 1] = plane
            planes.append(plane)
        pack_heat(3, j, planes)

    round_2.start()
    round_2.wait()

    @pl.loop(0, heat_x // block_t)
    def _(j):
        for x, plane in stepped(3, temp2, j):
            temp0[x + 1] = plane

    store_temp = pltpu.make_async_copy(temp0.at[pl.ds(1, heat_x)], out_hbm, load_sems.at[9])
    store_temp.start()
    for each in (round0, round1, round_k, round_1, round_2):
        each.drain()

    everyone = sent.at[pl.ds(0, group - 1)]
    pltpu.make_async_remote_copy(
        src_ref=everyone, dst_ref=everyone, send_sem=slot_send, recv_sem=slot_recv.at[0],
        device_id={"gx": wrap(ix + 1, n_gx)}, device_id_type=MESH,
    ).wait_send()
    store_potential.wait()
    store_temp.wait()


def shards(vec_prev, source, mag_mat, send_idx, send_count, recv_cell, temp, heat_mat):
    _, size_x, size_y, size_z = vec_prev.shape
    heat_x, heat_y, heat_z = temp.shape
    n_gx, n_gy = lax.axis_size("gx"), lax.axis_size("gy")
    group = n_gx * n_gy
    per = min(2, n_gx) * n_gy
    vmem = pltpu.VMEM
    anywhere = pl.BlockSpec(memory_space=pl.ANY)
    return pl.pallas_call(
        kernel,
        out_shape=(
            jax.ShapeDtypeStruct(vec_prev.shape, f32),
            jax.ShapeDtypeStruct(temp.shape, f32),
        ),
        in_specs=[anywhere] * 8,
        out_specs=(anywhere, anywhere),
        scratch_shapes=[
            vmem((2, size_x + 2, size_y, size_z), f32),
            vmem((2, size_x + 2, size_y, size_z), f32),
            vmem(source.shape, f32),
            vmem(mag_mat.shape, jnp.int32),
            vmem(send_idx.shape[1:], jnp.int32),
            pltpu.SMEM(send_count.shape, jnp.int32),
            vmem(recv_cell.shape[1:], jnp.int32),
            vmem((heat_x + 2, heat_y, heat_z), f32),
            vmem((heat_x + 2, heat_y, heat_z), f32),
            vmem((heat_x + 2, heat_y, heat_z), f32),
            vmem(heat_mat.shape, jnp.int32),
            vmem((heat_x + 2, heat_y, heat_z), f32),
            vmem((7, heat_x, heat_y, heat_z), f32),
            vmem((heat_x, heat_y, heat_z), f32),
            vmem((2, 2, 2, size_x, 1, size_z), f32),
            vmem((2, 2, 2, size_x, 1, size_z), f32),
            vmem((2, 2, 2, size_x * size_y // LANES, 1, LANES), f32),
            vmem((2, 2, 2, size_x * size_y // LANES, 1, LANES), f32),
            vmem((4, 2, heat_x, 1, heat_z), f32),
            vmem((4, 2, heat_x, 1, heat_z), f32),
            vmem((4, 2, heat_x * heat_y // LANES, 1, LANES), f32),
            vmem((4, 2, heat_x * heat_y // LANES, 1, LANES), f32),
            vmem((2 * size_z, size_x * size_y), bf16),
            vmem((size_x * size_y, n_gy * LANES), bf16),
            vmem((group, 1, LANES), f32),
            vmem((group, 1, LANES), f32),
            vmem((heat_x * heat_y, per * LANES), bf16),
            vmem((heat_z, per * LANES), bf16),
            vmem((heat_z, per * LANES), bf16),
            vmem((heat_x * heat_y, heat_z), f32),
            pltpu.SemaphoreType.DMA((10,)),
            pltpu.SemaphoreType.DMA((6, 6)),
            pltpu.SemaphoreType.DMA((6, 6)),
            pltpu.SemaphoreType.DMA,
            pltpu.SemaphoreType.DMA((n_gx,)),
        ],
        compiler_params=pltpu.CompilerParams(
            collective_id=0, has_side_effects=True, vmem_limit_bytes=56 << 20
        ),
    )(vec_prev, source, mag_mat, send_idx, send_count, recv_cell, temp, heat_mat)


def solution(mesh):
    placed = (
        P(None, "gx", "gy", "gz"),
        P(None, "gx", "gy", "gz"),
        P("gx", "gy", "gz"),
        P(("gx", "gy", "gz"), None, None),
        P(("gx", "gy", "gz"), None),
        P(("gx", "gy", "gz"), None, None),
        P("gx", "gy", "gz"),
        P("gx", "gy", "gz"),
    )
    return jax.shard_map(
        shards,
        mesh=mesh,
        in_specs=placed,
        out_specs=(P(None, "gx", "gy", "gz"), P("gx", "gy", "gz")),
        check_vma=False,
    )
```

time: 79.2 us -> 60.2 us (0.76)
  Pallas kernels: 74.5 us -> 55.4 us
    pallas_call x1, Pallas kernels: 74.5 us -> 55.4 us  [shards(): pl.pallas_call(kernel, out_shape=(jax.ShapeDtypeStruct(vec_prev.shape, f3...]
where the time goes in v2:
time: 60.2 us; the launch traced here: 59.9 us
  Pallas kernels  55.4 us (92%)
  local copies, waits for them, and re-layouts  3.9 us (6%)
  between operations  0.65 us (1%)
    pallas_call x1, Pallas kernels, shards(): pl.pallas_call(kernel, out_shape=(jax.ShapeDtypeStruct(vec_prev.shape, f3...  55.4 us
    unnamed x4, local copies, waits for them, and re-layouts  3.9 us

profile of v2, /device:TPU:8, one launch (start us, length us, event | category | flops | bytes accessed | tf_op | source)
XLA Modules:
  0.0 59.9 jit_solution(9933563608282663999)
XLA Ops:
  0.6 55.4 %shard_map.95 = (f32[2,128,16,128]{3,2,1,0:T(8,128)}, f32[32,16,256]{2,1,0:T(8,128)}) custom-call(f32[2,128,16,128]{3,2,1,0:T(8,128)} %vec_hbm.1, f32[2,128,16,128]{3,2,1,0:T(8,128)} %source_hbm.1, s32[128,16,128]{2,1,0:T(8,128)} %mag_hbm.1, s32[1,64,128]{2,1,0:T(8,128)} %idx_hbm.1, s32[1,64]{1,0:T(1,128)} %count_hbm.1, s32[1,64,128]{2,1,0:T(8,128)} %cell_hbm.1, ...), custom_call_target="tpu_custom_call" | custom-call | tf_op jit(solution)/shard_map/pallas_call | solution.py:479
  56.0 0.0 copy-start
  56.0 3.1 %copy.12 = f32[2,128,16,128]{3,2,1,0:T(8,128)} copy(f32[2,128,16,128]{3,2,1,0:T(8,128)} %get-tuple-element.4) | data formatting | bytes 4194304
  59.1 0.0 copy-done
  59.1 0.8 %copy.13 = f32[32,16,256]{2,1,0:T(8,128)} copy(f32[32,16,256]{2,1,0:T(8,128)S(1)} %copy-done) | data formatting | bytes 1048576
Async XLA Ops:
  56.0 3.1 %copy-start = (f32[32,16,256]{2,1,0:T(8,128)S(1)}, f32[32,16,256]{2,1,0:T(8,128)}, u32[]{:S(2)}) copy-start(f32[32,16,256]{2,1,0:T(8,128)} %get-tuple-element.5) | copy-start | bytes 1572868
